TPU v7x, 256 devices: a whole 4x4x8 slice. The times are simulated.
256 devices in a mesh: cable: 64 (over z_lo, y, x), freq: 4 (over z_hi, core).
Axes of the slice: x: 4, y: 4, z: 8 (z_hi: 2, z_lo: 4; z = z_hi * 4 + z_lo), core: 2. Of those that a mesh axis runs over, the one named last changes fastest.
Arguments:
- spectra: bfloat16 [2, 24576, 512], P(None, 'cable', 'freq'), may hold values from -6 to 6
- slow_bins: int32 [192, 16384], P(None, 'cable'), may hold values from 0 to 199
- weight_steps: int32 [192, 16384], P(None, 'cable'), may hold values from 0 to 64
- delays: int32 [192, 16384], P(None, 'cable'), may hold values from 0 to 1999
Outputs:
- node_spectra: float32 [16384, 2, 512], P('cable', None, 'freq')
- beam_power: float32 [16384], P('cable')
Inputs may be any that keep to these rules, and one draw needn't show every extreme that they name: `slow_bins`: the bin and the bin above it are both slownesses.
All inputs are finite; a program needn't handle non-finite values.
Results may differ from a plain program's by a relative error of at most 0.0035.
Values may be sent and summed in bfloat16 or wider, within the bound.
A program may use at most 192 MiB of HBM per device.

v0:
```python
import math

import jax
import jax.numpy as jnp
from jax import lax
from jax.sharding import PartitionSpec as P

SUB_LEN = 256
SLOW = 201
NT = 2000
BIN0 = 20
WSTEPS = 64


def passed_along(value, axis, by):
    peers = lax.axis_size(axis)
    pairs = [(i, i + by) for i in range(peers) if 0 <= i + by < peers]
    return lax.ppermute(value, axis, pairs)


def steering_table(freq_bins):
    offsets = jnp.arange(SUB_LEN, dtype=jnp.int32)
    slowness = jnp.arange(SLOW, dtype=jnp.int32) - SLOW // 2
    product = freq_bins[:, None, None] * offsets[None, :, None] * slowness[None, None, :]
    modulus = 50 * NT
    angles = jnp.mod(product, modulus).astype(jnp.float32) * (2.0 * math.pi / modulus)
    factor = SUB_LEN ** (-0.5)
    cosine = jnp.cos(angles) * factor
    sine = jnp.sin(angles) * factor
    upper_rows = jnp.concatenate([cosine, -sine], axis=2)
    lower_rows = jnp.concatenate([sine, cosine], axis=2)
    return jnp.concatenate([upper_rows, lower_rows], axis=1).astype(jnp.bfloat16)


def subarray_frames(extended, stride_len):
    channel_len = extended.shape[1] - stride_len
    sub_count = channel_len // stride_len
    freq_len = extended.shape[2]
    first_half = extended[:, :channel_len].reshape(2, sub_count, stride_len, freq_len)
    second_half = extended[:, stride_len:].reshape(2, sub_count, stride_len, freq_len)
    frames = jnp.concatenate([first_half, second_half], axis=2)
    return jnp.transpose(frames, (1, 0, 2, 3)).reshape(sub_count, 2 * SUB_LEN, freq_len)


def slant_stack(frames, freq_bins):
    sub_count, row_len, freq_len = frames.shape
    block_len = min(16, freq_len)
    num_blocks = freq_len // block_len
    blocked = jnp.transpose(frames.reshape(sub_count, row_len, num_blocks, block_len), (2, 0, 1, 3))
    bins_blocked = freq_bins.reshape(num_blocks, block_len)

    def one_block(operands):
        frame_block, bin_block = operands
        weights = steering_table(bin_block)
        stacked = jnp.einsum(
            "amf,fmq->faq", frame_block, weights, preferred_element_type=jnp.float32
        )
        stacked = stacked.astype(jnp.bfloat16).reshape(block_len, sub_count, 2, SLOW)
        return jnp.transpose(stacked, (1, 3, 2, 0))

    result = lax.map(one_block, (blocked, bins_blocked))
    return jnp.transpose(result, (1, 2, 3, 0, 4)).reshape(sub_count, SLOW, 2, freq_len)


def project_nodes(beam_table, bin_table, step_table, delay_table, freq_bins):
    sub_count = beam_table.shape[0]
    freq_len = beam_table.shape[3]
    columns = jnp.arange(SLOW, dtype=jnp.int32)[None, None, :]
    fraction = (step_table.astype(jnp.float32) / WSTEPS)[:, :, None]
    lower_hit = (columns == bin_table[:, :, None]).astype(jnp.float32)
    upper_hit = (columns == bin_table[:, :, None] + 1).astype(jnp.float32)
    interp = (lower_hit * (1.0 - fraction) + upper_hit * fraction).astype(jnp.bfloat16)
    flat_beams = beam_table.reshape(sub_count, SLOW, 2 * freq_len)
    value = jnp.einsum("anj,ajc->anc", interp, flat_beams, preferred_element_type=jnp.float32)
    value = value.reshape(sub_count, bin_table.shape[1], 2, freq_len)
    phase_index = jnp.mod(delay_table[:, :, None] * freq_bins[None, None, :], NT)
    phase = phase_index.astype(jnp.float32) * (2.0 * math.pi / NT)
    cosine = jnp.cos(phase)
    sine = jnp.sin(phase)
    real_part = value[:, :, 0] * cosine - value[:, :, 1] * sine
    imag_part = value[:, :, 0] * sine + value[:, :, 1] * cosine
    return jnp.stack([jnp.sum(real_part, axis=0), jnp.sum(imag_part, axis=0)], axis=1)


def fold_subarrays(running, beam_table, bin_table, step_table, delay_table, freq_bins):
    sub_count = beam_table.shape[0]
    block_len = math.gcd(sub_count, 8)
    num_blocks = sub_count // block_len

    def regroup(table):
        return table.reshape((num_blocks, block_len) + table.shape[1:])

    def one_step(carried, operands):
        beam_block, bin_block, step_block, delay_block = operands
        return (
            carried + project_nodes(beam_block, bin_block, step_block, delay_block, freq_bins),
            None,
        )

    result, unused = lax.scan(
        one_step,
        running,
        (regroup(beam_table), regroup(bin_table), regroup(step_table), regroup(delay_table)),
    )
    return result


def shards(spectra, slow_bins, weight_steps, delays):
    stride_len = SUB_LEN // 2
    freq_len = spectra.shape[2]
    total_subs = slow_bins.shape[0]
    node_len = slow_bins.shape[1]
    freq_bins = BIN0 + lax.axis_index("freq") * freq_len + jnp.arange(freq_len, dtype=jnp.int32)
    running = jnp.zeros((node_len, 2, freq_len), jnp.float32)
    border = passed_along(spectra[:, :stride_len], "cable", -1)
    extended = jnp.concatenate([spectra, border], axis=1)
    own_beams = slant_stack(subarray_frames(extended, stride_len), freq_bins)
    total = fold_subarrays(
        running,
        lax.all_gather(own_beams, "cable", axis=0, tiled=True),
        slow_bins,
        weight_steps,
        delays,
        freq_bins,
    )
    node_spectra = total * total_subs ** (-0.5)
    local_power = jnp.sum(node_spectra * node_spectra, axis=(1, 2)) / (
        freq_len * lax.axis_size("freq")
    )
    beam_power = lax.psum(local_power, "freq")
    return (node_spectra, beam_power)


def solution(mesh):
    placed = (P(None, "cable", "freq"), P(None, "cable"), P(None, "cable"), P(None, "cable"))
    return jax.shard_map(
        shards,
        mesh=mesh,
        in_specs=placed,
        out_specs=(P("cable", None, "freq"), P("cable")),
        check_vma=False,
    )
```

profile of v0, /device:TPU:1, one launch (start us, length us, event | category | flops | bytes accessed | tf_op | source)
XLA Modules:
  0.0 811.1 jit_solution(14880526310046978410)
XLA Ops:
  10.5 3.2 collective-permute-done
  15.4 148.5 %while.25 = (s32[]{:T(128)}, bf16[8,3,201,2,16]{2,3,4,1,0:T(2,128)(2,1)S(1)}, bf16[8,3,512,16]{2,3,0,1:T(8,128)(2,1)S(1)}, s32[8,16]{1,0:T(8,128)S(1)}, s32[]{:T(128)}) while((s32[]{:T(128)}, bf16[8,3,201,2,16]{2,3,4,1,0:T(2,128)(2,1)S(1)}, bf16[8,3,512,16]{2,3,0,1:T(8,128)(2,1)S(1)}, s32[8,16]{1,0:T(8,128)S(1)}, s32[]{:T(128)}) %tuple.82), condition=%wide.region_1.2_spmd, body=%wide.region_0.1_spmd.sunk | while | flops 58477608 | bytes 10275729 | solution.py:61
  15.5 16.0 %negate_convert_fusion.2 = (bf16[16,256,201]{1,2,0:T(8,128)(2,1)S(1)}, bf16[16,256,201]{1,2,0:T(8,128)(2,1)S(1)}, bf16[16,256,201]{1,2,0:T(8,128)(2,1)S(1)}) fusion(s32[201]{0:T(256)S(1)} %iota_add_fusion.4, s32[16,256]{1,0:T(8,128)S(1)} %iota_multiply_fusion.2), kind=kLoop, calls=%fused_computation.12.clone.1 | loop fusion | flops 12349440 | bytes 4956964 | tf_op jit(solution)/shard_map/convert.5
  31.6 2.3 fusion.43
  34.1 16.0 %negate_convert_fusion.2 = (bf16[16,256,201]{1,2,0:T(8,128)(2,1)S(1)}, bf16[16,256,201]{1,2,0:T(8,128)(2,1)S(1)}, bf16[16,256,201]{1,2,0:T(8,128)(2,1)S(1)}) fusion(s32[201]{0:T(256)S(1)} %iota_add_fusion.4, s32[16,256]{1,0:T(8,128)S(1)} %iota_multiply_fusion.2), kind=kLoop, calls=%fused_computation.12.clone.1 | loop fusion | flops 12349440 | bytes 4956964 | tf_op jit(solution)/shard_map/convert.5
  50.1 2.3 fusion.43
  52.7 16.0 %negate_convert_fusion.2 = (bf16[16,256,201]{1,2,0:T(8,128)(2,1)S(1)}, bf16[16,256,201]{1,2,0:T(8,128)(2,1)S(1)}, bf16[16,256,201]{1,2,0:T(8,128)(2,1)S(1)}) fusion(s32[201]{0:T(256)S(1)} %iota_add_fusion.4, s32[16,256]{1,0:T(8,128)S(1)} %iota_multiply_fusion.2), kind=kLoop, calls=%fused_computation.12.clone.1 | loop fusion | flops 12349440 | bytes 4956964 | tf_op jit(solution)/shard_map/convert.5
  68.7 2.3 fusion.43
  71.2 16.0 %negate_convert_fusion.2 = (bf16[16,256,201]{1,2,0:T(8,128)(2,1)S(1)}, bf16[16,256,201]{1,2,0:T(8,128)(2,1)S(1)}, bf16[16,256,201]{1,2,0:T(8,128)(2,1)S(1)}) fusion(s32[201]{0:T(256)S(1)} %iota_add_fusion.4, s32[16,256]{1,0:T(8,128)S(1)} %iota_multiply_fusion.2), kind=kLoop, calls=%fused_computation.12.clone.1 | loop fusion | flops 12349440 | bytes 4956964 | tf_op jit(solution)/shard_map/convert.5
  87.3 2.3 fusion.43
  89.8 16.0 %negate_convert_fusion.2 = (bf16[16,256,201]{1,2,0:T(8,128)(2,1)S(1)}, bf16[16,256,201]{1,2,0:T(8,128)(2,1)S(1)}, bf16[16,256,201]{1,2,0:T(8,128)(2,1)S(1)}) fusion(s32[201]{0:T(256)S(1)} %iota_add_fusion.4, s32[16,256]{1,0:T(8,128)S(1)} %iota_multiply_fusion.2), kind=kLoop, calls=%fused_computation.12.clone.1 | loop fusion | flops 12349440 | bytes 4956964 | tf_op jit(solution)/shard_map/convert.5
  105.8 2.3 fusion.43
  108.4 16.0 %negate_convert_fusion.2 = (bf16[16,256,201]{1,2,0:T(8,128)(2,1)S(1)}, bf16[16,256,201]{1,2,0:T(8,128)(2,1)S(1)}, bf16[16,256,201]{1,2,0:T(8,128)(2,1)S(1)}) fusion(s32[201]{0:T(256)S(1)} %iota_add_fusion.4, s32[16,256]{1,0:T(8,128)S(1)} %iota_multiply_fusion.2), kind=kLoop, calls=%fused_computation.12.clone.1 | loop fusion | flops 12349440 | bytes 4956964 | tf_op jit(solution)/shard_map/convert.5
  124.4 2.3 fusion.43
  126.9 16.0 %negate_convert_fusion.2 = (bf16[16,256,201]{1,2,0:T(8,128)(2,1)S(1)}, bf16[16,256,201]{1,2,0:T(8,128)(2,1)S(1)}, bf16[16,256,201]{1,2,0:T(8,128)(2,1)S(1)}) fusion(s32[201]{0:T(256)S(1)} %iota_add_fusion.4, s32[16,256]{1,0:T(8,128)S(1)} %iota_multiply_fusion.2), kind=kLoop, calls=%fused_computation.12.clone.1 | loop fusion | flops 12349440 | bytes 4956964 | tf_op jit(solution)/shard_map/convert.5
  143.0 2.3 fusion.43
  145.5 16.0 %negate_convert_fusion.2 = (bf16[16,256,201]{1,2,0:T(8,128)(2,1)S(1)}, bf16[16,256,201]{1,2,0:T(8,128)(2,1)S(1)}, bf16[16,256,201]{1,2,0:T(8,128)(2,1)S(1)}) fusion(s32[201]{0:T(256)S(1)} %iota_add_fusion.4, s32[16,256]{1,0:T(8,128)S(1)} %iota_multiply_fusion.2), kind=kLoop, calls=%fused_computation.12.clone.1 | loop fusion | flops 12349440 | bytes 4956964 | tf_op jit(solution)/shard_map/convert.5
  161.5 2.3 fusion.43
  165.1 354.0 %all-gather.2.cloned.1.call-done = bf16[192,201,2,128]{3,2,1,0:T(2,128)(2,1)} async-done(((bf16[3,201,2,128]{3,2,1,0:T(2,128)(2,1)}), bf16[192,201,2,128]{3,2,1,0:T(2,128)(2,1)}) %all-gather.2.cloned.1.call-update) | async-done | bytes 19759120 | tf_op jit(solution)/shard_map/all_gather | solution.py:120
  519.1 234.2 %while.26 = (s32[]{:T(128)}, f32[256,2,128]{0,2,1:T(8,128)S(1)}, s32[24,8,256]{2,1,0:T(8,128)}, s32[24,8,256]{2,1,0:T(8,128)}, bf16[24,8,201,2,128]{4,3,2,1,0:T(...) while((s32[]{:T(128)}, f32[256,2,128]{0,2,1:T(8,128)S(1)}, ...), condition=%wide.region_5.6_spmd.clone, body=%wide.region_2.5_spmd.clone.sunk | while | flops 217829504 | bytes 9467003 | solution.py:100
  520.5 1.7 constant_dynamic-slice_fusion.6
  523.8 4.9 subtract_reduce_fusion.2
  530.3 1.7 constant_dynamic-slice_fusion.6
  533.6 4.9 subtract_reduce_fusion.2
  543.3 4.9 subtract_reduce_fusion.2
  553.1 4.9 subtract_reduce_fusion.2
  559.6 1.7 constant_dynamic-slice_fusion.6
  562.9 4.9 subtract_reduce_fusion.2
  572.6 4.9 subtract_reduce_fusion.2
  582.4 4.9 subtract_reduce_fusion.2
  592.1 4.9 subtract_reduce_fusion.2
  601.9 4.9 subtract_reduce_fusion.2
  611.7 4.9 subtract_reduce_fusion.2
  621.4 4.9 subtract_reduce_fusion.2
  631.2 4.9 subtract_reduce_fusion.2
  640.9 4.9 subtract_reduce_fusion.2
  650.7 4.9 subtract_reduce_fusion.2
  660.4 4.9 subtract_reduce_fusion.2
  670.2 4.9 subtract_reduce_fusion.2
  680.0 4.9 subtract_reduce_fusion.2
  689.7 4.9 subtract_reduce_fusion.2
  699.5 4.9 subtract_reduce_fusion.2
  709.2 4.9 subtract_reduce_fusion.2
  719.0 4.9 subtract_reduce_fusion.2
  728.8 4.9 subtract_reduce_fusion.2
  738.5 4.9 subtract_reduce_fusion.2
  748.3 4.9 subtract_reduce_fusion.2
  755.0 49.3 %psum.7 = f32[256]{0:T(256)} all-reduce(f32[256]{0:T(256)S(1)} %broadcast_multiply_fusion.1), channel_id=1, replica_groups=mesh['cable'=64,'freq'=4] {'freq'}, use_global_device_ids=true, to_apply=%region_7.8 | all-reduce | flops 256 | bytes 2048 | tf_op jit(solution)/shard_map/psum | solution.py:130
  (254 shorter events, 119.3 us)
Async XLA Ops:
  7.2 512.0 %all-gather.2.cloned.1.call-start = ((), (), s32[]{:S(2)}) async-start(), calls=%async_computation | async-start | bytes 20067840 | tf_op jit(solution)/shard_map/all_gather | solution.py:120
  8.1 5.6 collective-permute-start
Sparse Core Ops, SparseCore 0:
  165.3 353.8 all-gather.1
where the time goes:
time: 816 us; the launch traced here: 811 us
  waiting for transfers between devices  357 us (44%)
  other arithmetic  285 us (35%)
  local copies, waits for them, and re-layouts  66.6 us (8%)
  blocking collectives  49.3 us (6%)
  matrix products  35.5 us (4%)
  between operations  14.1 us (2%)
    all_gather x1, waiting for transfers between devices, shards(): lax.all_gather(own_beams, 'cable', axis=0, tiled=True)  354 us
    another operation x8, other arithmetic  128 us
    reduce_sum x24, other arithmetic, project_nodes(): jnp.sum(real_part, axis=0)  118 us
    psum x1, blocking collectives, shards(): beam_power = lax.psum(local_power, 'freq')  49.3 us
    dynamic_slice x48, local copies, waits for them, and re-layouts, fold_subarrays(): lax.scan(one_step, running, (regroup(beam_table), regroup(bin_table), reg...  44.5 us
    dot_general x8, matrix products, one_block(): jnp.einsum('amf,fmq->faq', frame_block, weights, preferred_element_type=j...  18 us
    dot_general x24, matrix products, project_nodes(): jnp.einsum('anj,ajc->anc', interp, flat_beams, preferred_element_type=jnp...  17.5 us
    sub x24, other arithmetic, project_nodes(): 1.0 - fraction  16.9 us
  transfers between devices with their start and end apart: 2, of which 2 were waited for; matrix products, arithmetic and copies ran while one was open for 0% of the time, Pallas kernels for 0%

commit v1 on v0

v1 whole, which is shorter than its diff:
```python
import functools
import math

import jax
import jax.numpy as jnp
import numpy as np
from jax import lax
from jax.experimental import pallas as pl
from jax.experimental.pallas import tpu as pltpu
from jax.sharding import PartitionSpec as P

SUB_LEN = 256
SLOW = 201
NT = 2000
BIN0 = 20
WSTEPS = 64
HALF = SLOW // 2
STRIDE = SUB_LEN // 2

Z, Y, X = 4, 4, 4
PLANE = Y * X
FREQ_DEV = 4
F = 128
N = 256
BLOCKS = 3
SHARD = BLOCKS * 2 * F
LOCAL = BLOCKS * PLANE
ROWS = LOCAL + 1
PAD_ROWS = 56
FT = F // 8
GROUP = 7
MESH = pl.DeviceIdType.MESH


def power_series(fun, degree):
    fit = np.polynomial.chebyshev.Chebyshev.interpolate(fun, degree, domain=[0.0, 0.25])
    return [float(c) for c in fit.convert(kind=np.polynomial.Polynomial, domain=[-1, 1], window=[-1, 1]).coef]


COS_TERMS = power_series(lambda v: np.cos(2 * np.pi * np.sqrt(v)), 7)
SIN_TERMS = power_series(lambda v: 2 * np.pi * np.sinc(2 * np.sqrt(v)), 6)


def horner(v, terms):
    total = jnp.full_like(v, terms[-1])
    for term in terms[-2::-1]:
        total = total * v + term
    return total


def unit_circle(count, period):
    rest = count - jnp.round(count * (1.0 / period)) * period
    turns = rest * (1.0 / period)
    v = turns * turns
    return horner(v, COS_TERMS), horner(v, SIN_TERMS) * turns


def places():
    cable = lax.axis_index("cable")
    z = cable // PLANE
    y = (cable // X) % Y
    x = cable % X
    return z, y, x


def cable_id(z, y, x):
    return {"cable": (z * Y + y) * X + x}


def steering(f, first_bin, table):
    period = float(50 * NT)
    bins = (first_bin + f).astype(jnp.float32)
    k = lax.broadcasted_iota(jnp.int32, (8, 128), 0).astype(jnp.float32)
    s = lax.broadcasted_iota(jnp.int32, (8, 128), 1).astype(jnp.float32)
    bs = s * bins
    cos0, sin0 = unit_circle(bs * k, period)
    cos8, sin8 = unit_circle(bs * 8.0, period)
    factor = SUB_LEN ** -0.5
    cos0, sin0 = cos0 * factor, sin0 * factor
    cos1, sin1 = cos0 * cos8 - sin0 * sin8, sin0 * cos8 + cos0 * sin8
    twice = cos8 + cos8
    for step in range(SUB_LEN // 16):
        rows = pl.ds(step * 16, 16)
        table[f, rows, 0:128] = jnp.concatenate([cos0, cos1], axis=0).astype(jnp.bfloat16)
        table[f, rows, 128:256] = jnp.concatenate([sin0, sin1], axis=0).astype(jnp.bfloat16)
        cos0, sin0 = twice * cos1 - cos0, twice * sin1 - sin0
        cos1, sin1 = twice * cos0 - cos1, twice * sin0 - sin1


def widen(gathered, wide):
    per = 2 * F
    wide[0:per] = jnp.zeros((per, 128), jnp.float32)
    wide[(LOCAL + 1) * per:(LOCAL + 2) * per] = jnp.zeros((per, 128), jnp.float32)

    def one(block, carry):
        rows = pl.multiple_of(block * per, per)
        wide[pl.ds(rows + per, per)] = gathered[pl.ds(rows, per)].astype(jnp.float32)
        return carry

    lax.fori_loop(0, LOCAL, one, 0)


def stack_tile(tile, wide, table, plus, minus, beams):
    per = 2 * F
    for f0 in range(8):
        f = tile * 8 + f0
        parts = []
        for c in range(2):
            left = wide[pl.ds(c * F + f, PAD_ROWS, stride=per), :]
            right = wide[pl.ds(per + c * F + f, PAD_ROWS, stride=per), :]
            parts.append(jnp.concatenate([left, right], axis=1))
        frames = jnp.concatenate(parts, axis=0).astype(jnp.bfloat16)
        out = jnp.dot(frames, table[f], preferred_element_type=jnp.float32)
        a_re, b_re = out[:PAD_ROWS, :128], out[:PAD_ROWS, 128:]
        a_im, b_im = out[PAD_ROWS:, :128], out[PAD_ROWS:, 128:]
        plus[pl.ds(f0, PAD_ROWS, stride=16), :] = a_re + b_im
        plus[pl.ds(8 + f0, PAD_ROWS, stride=16), :] = a_im - b_re
        minus[pl.ds(f0, PAD_ROWS, stride=16), :] = a_re - b_im
        minus[pl.ds(8 + f0, PAD_ROWS, stride=16), :] = a_im + b_re
    rows = pl.ds(pl.multiple_of(tile * 16, 16), 16)
    beams[:, rows, 0:128] = plus[...].reshape(PAD_ROWS, 16, 128).astype(jnp.bfloat16)
    beams[:, rows, 128:256] = minus[...].reshape(PAD_ROWS, 16, 128).astype(jnp.bfloat16)


def project_one(m, r, first_bin, beams, slowness, tabs, eighth, total):
    def row(ref, *at):
        return jnp.broadcast_to(ref[at + (pl.ds(r, 1), slice(None))], (8, N))

    def packed(value):
        return jnp.concatenate([value, value], axis=0).astype(jnp.bfloat16)

    lower = packed(row(tabs, m, 0) - float(HALF))
    weight = row(tabs, m, 1) * (1.0 / WSTEPS)
    rising, falling = packed(1.0 - weight), packed(1.0 + weight)
    tiles = []
    for q in range(16):
        at = slowness[q * 16:(q + 1) * 16, :]
        gap = jnp.concatenate([at, at], axis=1) - lower
        tiles.append(jnp.maximum(jnp.minimum(gap + rising, falling - gap), jnp.bfloat16(0)))
    hat = jnp.concatenate(tiles, axis=0)
    value = jnp.dot(beams[r], hat, preferred_element_type=jnp.float32)
    bins = (first_bin + lax.broadcasted_iota(jnp.int32, (8, N), 0)).astype(jnp.float32)
    cos0, sin0 = unit_circle(row(tabs, m, 2) * bins, float(NT))
    cos8, sin8 = row(eighth, 0), row(eighth, 1)
    cos1, sin1 = cos0 * cos8 - sin0 * sin8, sin0 * cos8 + cos0 * sin8
    twice = cos8 + cos8
    for t in range(FT):
        re, im = value[t * 16:t * 16 + 8], value[t * 16 + 8:t * 16 + 16]
        total[t * 16:t * 16 + 8, :] += re * cos0 - im * sin0
        total[t * 16 + 8:t * 16 + 16, :] += re * sin0 + im * cos0
        cos0, sin0, cos1, sin1 = cos1, sin1, twice * cos1 - cos0, twice * sin1 - sin0


def kernel(spectra, slow_bins, weight_steps, delays, slowness, node_spectra, power,
           gathered, table, wide, plus, minus, beams, outgoing, tabs, eighth, total, sent, landed, mine, theirs,
           ag_send, ag_recv, tab_send, tab_recv, sum_send, sum_recv, pow_send, pow_recv):
    z, y, x = places()
    freq = lax.axis_index("freq")
    first_bin = BIN0 + freq * F
    barrier = pltpu.get_barrier_semaphore()
    greet = [cable_id(z, y, (x + 1) % X), cable_id(z, y, (x + X - 1) % X),
             cable_id(z, (y + 1) % Y, x), cable_id(z, (y + Y - 1) % Y, x)]
    greet += [cable_id((z + i) % Z, y, x) for i in range(1, Z)]
    greet += [{"freq": (freq + i) % FREQ_DEV} for i in range(1, FREQ_DEV)]
    for device in greet:
        pl.semaphore_signal(barrier, inc=1, device_id=device, device_id_type=MESH)

    own = y * X + x
    for b in range(BLOCKS):
        for c in range(2):
            block = spectra[c, b * STRIDE:(b + 1) * STRIDE, :].astype(jnp.float32)
            rows = pl.multiple_of(own * SHARD + (b * 2 + c) * F, F)
            gathered[pl.ds(rows, F), :] = block.T.astype(jnp.bfloat16)
    for i, source in enumerate((slow_bins, weight_steps, delays)):
        for to in range(Z):
            if to == 0:
                outgoing[0, i, 0:1, :] = jnp.full((1, N), -2000.0 if i == 0 else 0.0, jnp.float32)
                outgoing[0, i, 1:ROWS, :] = source[0:LOCAL, :].astype(jnp.float32)
            else:
                outgoing[to, i, 0:ROWS, :] = source[to * LOCAL - 1:(to + 1) * LOCAL, :].astype(jnp.float32)
            outgoing[to, i, ROWS:PAD_ROWS, :] = jnp.zeros((PAD_ROWS - ROWS, N), jnp.float32)
    pl.semaphore_wait(barrier, len(greet))

    half, quarter = SHARD // 2, SHARD // 4

    def shifted(way, dx, dy):
        if way == 0:
            return (y + Y + dy) % Y, (x + X + dx) % X
        return (y + Y + dx) % Y, (x + X + dy) % X

    def piece(way, owner, kind):
        start = (owner[0] * X + owner[1]) * SHARD + way * half
        size = half
        if kind == 2:
            size = quarter
        elif kind == 3:
            start, size = start + quarter, quarter
        return gathered.at[pl.ds(pl.multiple_of(start, quarter), size), :]

    started = []

    def send(way, stage, kind, owner):
        by = 1 if kind in (0, 2) else -1
        to = shifted(way, by, 0) if stage == 0 else shifted(way, 0, by)
        copy = pltpu.make_async_remote_copy(
            src_ref=piece(way, owner, kind), dst_ref=piece(way, owner, kind),
            send_sem=ag_send.at[way, stage, kind], recv_sem=ag_recv.at[way, stage, kind],
            device_id=cable_id(z, *to), device_id_type=MESH)
        copy.start()
        started.append(copy)

    def arrive(way, stage, kind, owner):
        pltpu.make_async_remote_copy(
            src_ref=piece(way, owner, kind), dst_ref=piece(way, owner, kind),
            send_sem=ag_send.at[way, stage, kind], recv_sem=ag_recv.at[way, stage, kind],
            device_id=cable_id(z, y, (x + 1) % X), device_id_type=MESH).wait_recv()

    first = {0: 0, 1: -1, 2: 1, 3: 2}

    for way in range(2):
        send(way, 0, 0, shifted(way, 0, 0))
        send(way, 0, 1, shifted(way, 0, 0))
    for way in range(2):
        send(way, 1, 0, shifted(way, 0, 0))
        send(way, 1, 1, shifted(way, 0, 0))

    tab_copies = []
    for i in range(1, Z):
        to = (z + i) % Z
        copy = pltpu.make_async_remote_copy(
            src_ref=outgoing.at[to], dst_ref=tabs.at[z],
            send_sem=tab_send.at[i - 1], recv_sem=tab_recv.at[i - 1],
            device_id=cable_id(to, y, x), device_id_type=MESH)
        copy.start()
        tab_copies.append(copy)
    tabs[z] = outgoing[z]

    def steer(part, parts):
        def one(f, carry):
            steering(f, first_bin, table)
            return carry

        lax.fori_loop(part * F // parts, (part + 1) * F // parts, one, 0)

    steer(0, 8)
    for way in range(2):
        for kind, j in ((0, 1), (1, 2)):
            owner = shifted(way, first[j], 0)
            arrive(way, 0, kind, owner)
            send(way, 0, 2 + kind, owner)
            send(way, 1 + j, 0, owner)
            send(way, 1 + j, 1, owner)
    steer(1, 8)
    for way in range(2):
        owner = shifted(way, 2, 0)
        arrive(way, 0, 2, owner)
        arrive(way, 0, 3, owner)
        send(way, 4, 0, owner)
        send(way, 4, 1, owner)
    for j in range(4):
        steer(2 + j, 8)
        for way in range(2):
            for kind, by in ((0, -1), (1, 1)):
                owner = shifted(way, first[j], by)
                arrive(way, 1 + j, kind, owner)
                send(way, 1 + j, 2 + kind, owner)
    steer(6, 8)
    steer(7, 8)
    for j in range(4):
        for way in range(2):
            owner = shifted(way, first[j], 2)
            arrive(way, 1 + j, 2, owner)
            arrive(way, 1 + j, 3, owner)

    widen(gathered, wide)

    def one_tile(tile, carry):
        stack_tile(tile, wide, table, plus, minus, beams)
        return carry

    lax.fori_loop(0, FT, one_tile, 0)

    for i in range(1, Z):
        pltpu.make_async_remote_copy(
            src_ref=outgoing.at[z], dst_ref=tabs.at[(z + Z - i) % Z],
            send_sem=tab_send.at[i - 1], recv_sem=tab_recv.at[i - 1],
            device_id=cable_id((z + i) % Z, y, x), device_id_type=MESH).wait_recv()

    sums = []
    for step in range(Z):
        m = (z + 1 + step) % Z
        cos8, sin8 = unit_circle(tabs[m, 2] * 8.0, float(NT))
        eighth[0] = cos8
        eighth[1] = sin8
        total[...] = jnp.zeros_like(total)

        def one_group(g, carry):
            for j in range(GROUP):
                project_one(m, g * GROUP + j, first_bin, beams, slowness, tabs, eighth, total)
            return carry

        lax.fori_loop(0, ROWS // GROUP, one_group, 0)
        if step < Z - 1:
            sent[step] = total[...]
            copy = pltpu.make_async_remote_copy(
                src_ref=sent.at[step], dst_ref=landed.at[step],
                send_sem=sum_send.at[step], recv_sem=sum_recv.at[step],
                device_id=cable_id(m, y, x), device_id_type=MESH)
            copy.start()
            sums.append(copy)

    for copy in sums:
        copy.wait_recv()
    result = (total[...] + landed[0] + landed[1] + landed[2]) * (Z * LOCAL) ** -0.5
    mine[...] = jnp.broadcast_to(jnp.sum(result * result, axis=0, keepdims=True), (8, N))
    power_copies = []
    for i in range(1, FREQ_DEV):
        copy = pltpu.make_async_remote_copy(
            src_ref=mine, dst_ref=theirs.at[i - 1],
            send_sem=pow_send.at[i - 1], recv_sem=pow_recv.at[i - 1],
            device_id={"freq": (freq + i) % FREQ_DEV}, device_id_type=MESH)
        copy.start()
        power_copies.append(copy)
    split = result.reshape(FT, 2, 8, N)
    for c in range(2):
        part = split[:, c].reshape(F, N)
        node_spectra[:, c, :] = part.T
    for copy in power_copies:
        copy.wait_recv()
    power[...] = (mine[0:1] + theirs[0, 0:1] + theirs[1, 0:1] + theirs[2, 0:1]) * (1.0 / (F * FREQ_DEV))
    for copy in started + tab_copies + sums + power_copies:
        copy.wait_send()


def slowness_rows():
    s = np.full((256, 128), 4000.0, np.float32)
    s[0:HALF + 1] = np.arange(HALF + 1)[:, None]
    s[129:129 + HALF] = -np.arange(1, HALF + 1)[:, None]
    return jnp.asarray(s, jnp.bfloat16)


def shards(spectra, slow_bins, weight_steps, delays):
    vmem = pl.BlockSpec(memory_space=pltpu.VMEM)
    f32, bf16, dma = jnp.float32, jnp.bfloat16, pltpu.SemaphoreType.DMA
    node_spectra, power = pl.pallas_call(
        kernel,
        out_shape=(jax.ShapeDtypeStruct((N, 2, F), f32), jax.ShapeDtypeStruct((1, N), f32)),
        in_specs=[vmem] * 5,
        out_specs=(vmem, vmem),
        scratch_shapes=[
            pltpu.VMEM((PLANE * SHARD, 128), bf16),
            pltpu.VMEM((F, 256, 256), bf16),
            pltpu.VMEM(((PAD_ROWS + 1) * 2 * F, 128), f32),
            pltpu.VMEM((PAD_ROWS * 16, 128), f32),
            pltpu.VMEM((PAD_ROWS * 16, 128), f32),
            pltpu.VMEM((PAD_ROWS, 2 * F, 256), bf16),
            pltpu.VMEM((Z, 3, PAD_ROWS, N), f32),
            pltpu.VMEM((Z, 3, PAD_ROWS, N), f32),
            pltpu.VMEM((2, PAD_ROWS, N), f32),
            pltpu.VMEM((2 * F, N), f32),
            pltpu.VMEM((Z - 1, 2 * F, N), f32),
            pltpu.VMEM((Z - 1, 2 * F, N), f32),
            pltpu.VMEM((8, N), f32),
            pltpu.VMEM((FREQ_DEV - 1, 8, N), f32),
            dma((2, 5, 4)),
            dma((2, 5, 4)),
            dma((Z - 1,)),
            dma((Z - 1,)),
            dma((Z - 1,)),
            dma((Z - 1,)),
            dma((FREQ_DEV - 1,)),
            dma((FREQ_DEV - 1,)),
        ],
        compiler_params=pltpu.CompilerParams(
            collective_id=0, has_side_effects=True, vmem_limit_bytes=60 * 1024 * 1024
        ),
    )(spectra, slow_bins, weight_steps, delays, slowness_rows())
    return node_spectra, power.reshape(N)


def solution(mesh):
    placed = (P(None, "cable", "freq"), P(None, "cable"), P(None, "cable"), P(None, "cable"))
    return jax.shard_map(
        shards,
        mesh=mesh,
        in_specs=placed,
        out_specs=(P("cable", None, "freq"), P("cable")),
        check_vma=False,
    )
```

time: 816 us -> 83.7 us (0.10)
  the two profiles are of different devices: /device:TPU:1 before, /device:TPU:33 now
where the time goes in v1:
time: 83.7 us; the launch traced here: 83.6 us
  Pallas kernels  80.7 us (96%)
  local copies, waits for them, and re-layouts  2.24 us (3%)
    pallas_call x1, Pallas kernels, shards(): pl.pallas_call(kernel, out_shape=(jax.ShapeDtypeStruct((N, 2, F), f32), j...  80.7 us
    unnamed x4, local copies, waits for them, and re-layouts  2.24 us

profile of v1, /device:TPU:33, one launch (start us, length us, event | category | flops | bytes accessed | tf_op | source)
XLA Modules:
  0.0 83.6 jit_solution(13427854273692600982)
XLA Ops:
  0.6 80.7 %shard_map.68 = (f32[256,2,128]{2,1,0:T(2,128)}, f32[1,256]{1,0:T(1,128)}) custom-call(bf16[2,384,128]{2,1,0:T(8,128)(2,1)} %spectra.1, s32[192,256]{1,0:T(8,128)} %slow_bins.1, s32[192,256]{1,0:T(8,128)} %weight_steps.1, s32[192,256]{1,0:T(8,128)} %delays.1, bf16[256,128]{1,0:T(8,128)(2,1)} %constant.2.clone.slowness), custom_call_target="tpu_custom_call" | custom-call | tf_op jit(solution)/shard_map/pallas_call | solution.py:345
  81.4 0.0 copy-start
  81.4 1.7 %copy.9 = f32[256,2,128]{2,1,0:T(2,128)} copy(f32[256,2,128]{2,1,0:T(2,128)} %get-tuple-element.8) | data formatting | bytes 524288
  83.0 0.0 copy-done
  83.0 0.6 copy.10
Async XLA Ops:
  81.4 1.7 %copy-start = (f32[1,256]{1,0:T(1,128)S(1)}, f32[1,256]{1,0:T(1,128)}, u32[]{:S(2)}) copy-start(f32[1,256]{1,0:T(1,128)} %get-tuple-element.5) | copy-start | bytes 3076

commit v2 on v1

v2 whole, which is shorter than its diff:
```python
import functools
import math

import jax
import jax.numpy as jnp
import numpy as np
from jax import lax
from jax.experimental import pallas as pl
from jax.experimental.pallas import tpu as pltpu
from jax.sharding import PartitionSpec as P

SUB_LEN = 256
SLOW = 201
NT = 2000
BIN0 = 20
WSTEPS = 64
HALF = SLOW // 2
STRIDE = SUB_LEN // 2

Z, Y, X = 4, 4, 4
PLANE = Y * X
FREQ_DEV = 4
F = 128
N = 256
BLOCKS = 3
SHARD = BLOCKS * 2 * F
LOCAL = BLOCKS * PLANE
ROWS = LOCAL + 1
PAD_ROWS = 56
FT = F // 8
CHUNKS = 2
CF = F // CHUNKS
CT = CF // 8
CROWS = SHARD // CHUNKS
PER = 2 * CF + 8
STEP = 24
WIDE = 4
TAB_ROWS = 64
GROUP = 7
MESH = pl.DeviceIdType.MESH


def power_series(fun, degree):
    fit = np.polynomial.chebyshev.Chebyshev.interpolate(fun, degree, domain=[0.0, 0.25])
    return [float(c) for c in fit.convert(kind=np.polynomial.Polynomial, domain=[-1, 1], window=[-1, 1]).coef]


COS_TERMS = power_series(lambda v: np.cos(2 * np.pi * np.sqrt(v)), 7)
SIN_TERMS = power_series(lambda v: 2 * np.pi * np.sinc(2 * np.sqrt(v)), 6)


def horner(v, terms):
    total = jnp.full_like(v, terms[-1])
    for term in terms[-2::-1]:
        total = total * v + term
    return total


def unit_circle(count, period):
    rest = count - jnp.round(count * (1.0 / period)) * period
    turns = rest * (1.0 / period)
    v = turns * turns
    return horner(v, COS_TERMS), horner(v, SIN_TERMS) * turns


def places():
    cable = lax.axis_index("cable")
    z = cable // PLANE
    y = (cable // X) % Y
    x = cable % X
    return z, y, x


def cable_id(z, y, x):
    return {"cable": (z * Y + y) * X + x}


def steering(group, first_bin, table):
    period = float(50 * NT)
    k = lax.broadcasted_iota(jnp.int32, (8, 128), 0).astype(jnp.float32)
    s = lax.broadcasted_iota(jnp.int32, (8, 128), 1).astype(jnp.float32)
    factor = SUB_LEN ** -0.5
    state = []
    for u in range(WIDE):
        bs = s * (first_bin + group * WIDE + u).astype(jnp.float32)
        cos0, sin0 = unit_circle(bs * k, period)
        cos8, sin8 = unit_circle(bs * 8.0, period)
        cos0, sin0 = cos0 * factor, sin0 * factor
        state.append((cos0, sin0, cos0 * cos8 - sin0 * sin8, sin0 * cos8 + cos0 * sin8, cos8 + cos8))
    for step in range(SUB_LEN // 16):
        rows = pl.ds(step * 16, 16)
        for u in range(WIDE):
            cos0, sin0, cos1, sin1, twice = state[u]
            table[group * WIDE + u, rows, 0:128] = jnp.concatenate([cos0, cos1], axis=0).astype(jnp.bfloat16)
            table[group * WIDE + u, rows, 128:256] = jnp.concatenate([sin0, sin1], axis=0).astype(jnp.bfloat16)
            cos0, sin0 = twice * cos1 - cos0, twice * sin1 - sin0
            cos1, sin1 = twice * cos0 - cos1, twice * sin0 - sin1
            state[u] = cos0, sin0, cos1, sin1, twice


def widen(chunk, gathered, wide):
    wide[0:2 * CF] = jnp.zeros((2 * CF, 128), jnp.float32)
    wide[(LOCAL + 1) * PER:(LOCAL + 1) * PER + 2 * CF] = jnp.zeros((2 * CF, 128), jnp.float32)

    def one(device, carry):
        for b in range(BLOCKS):
            source = pl.multiple_of(device * SHARD + chunk * CROWS + b * 2 * CF, 2 * CF)
            target = pl.multiple_of((device * BLOCKS + b + 1) * PER, 8)
            wide[pl.ds(target, 2 * CF)] = gathered[pl.ds(source, 2 * CF)].astype(jnp.float32)
        return carry

    lax.fori_loop(0, PLANE, one, 0)


def stack_tile(chunk, tile, wide, table, plus, minus, beams):
    for f0 in range(8):
        at = tile * 8 + f0
        parts = []
        for c in range(2):
            left = wide[pl.ds(c * CF + at, PAD_ROWS, stride=PER), :]
            right = wide[pl.ds(PER + c * CF + at, PAD_ROWS, stride=PER), :]
            parts.append(jnp.concatenate([left, right], axis=1))
        frames = jnp.concatenate(parts, axis=0).astype(jnp.bfloat16)
        out = jnp.dot(frames, table[chunk * CF + at], preferred_element_type=jnp.float32)
        a_re, b_re = out[:PAD_ROWS, :128], out[:PAD_ROWS, 128:]
        a_im, b_im = out[PAD_ROWS:, :128], out[PAD_ROWS:, 128:]
        plus[pl.ds(f0, PAD_ROWS, stride=STEP), :] = a_re + b_im
        plus[pl.ds(8 + f0, PAD_ROWS, stride=STEP), :] = a_im - b_re
        minus[pl.ds(f0, PAD_ROWS, stride=STEP), :] = a_re - b_im
        minus[pl.ds(8 + f0, PAD_ROWS, stride=STEP), :] = a_im + b_re
    rows = pl.ds(pl.multiple_of((chunk * CT + tile) * 16, 16), 16)
    for side, sorted_beams in enumerate((plus, minus)):
        block = sorted_beams[...].reshape(PAD_ROWS, STEP, 128)[:ROWS, :16]
        beams[:, rows, side * 128:(side + 1) * 128] = block.astype(jnp.bfloat16)


def table_row(ref, r, *at):
    return jnp.broadcast_to(ref[at + (pl.ds(r, 1), slice(None))], (8, N))


def hat_of(m, r, slowness, tabs):
    def packed(value):
        return jnp.concatenate([value, value], axis=0).astype(jnp.bfloat16)

    lower = packed(table_row(tabs, r, m, 0) - float(HALF))
    weight = table_row(tabs, r, m, 1) * (1.0 / WSTEPS)
    rising, falling = packed(1.0 - weight), packed(1.0 + weight)
    tiles = []
    for q in range(16):
        at = slowness[q * 16:(q + 1) * 16, :]
        gap = jnp.concatenate([at, at], axis=1) - lower
        tiles.append(jnp.maximum(jnp.minimum(gap + rising, falling - gap), jnp.bfloat16(0)))
    return jnp.concatenate(tiles, axis=0)


def prepare_one(m, r, slot, first_bin, slowness, tabs, hats, starts):
    if slot is not None:
        hats[slot, r] = hat_of(m, r, slowness, tabs)
    bins = (first_bin + lax.broadcasted_iota(jnp.int32, (8, N), 0)).astype(jnp.float32)
    cos0, sin0 = unit_circle(table_row(tabs, r, m, 2) * bins, float(NT))
    starts[m, r, 0:8] = cos0
    starts[m, r, 8:16] = sin0


def project_one(m, r, hat, beams, starts, eighth, total):
    value = jnp.dot(beams[r], hat, preferred_element_type=jnp.float32)
    cos0, sin0 = starts[m, r, 0:8], starts[m, r, 8:16]
    cos8, sin8 = table_row(eighth, r, 0), table_row(eighth, r, 1)
    cos1, sin1 = cos0 * cos8 - sin0 * sin8, sin0 * cos8 + cos0 * sin8
    twice = cos8 + cos8
    for t in range(FT):
        re, im = value[t * 16:t * 16 + 8], value[t * 16 + 8:t * 16 + 16]
        total[t * 16:t * 16 + 8, :] += re * cos0 - im * sin0
        total[t * 16 + 8:t * 16 + 16, :] += re * sin0 + im * cos0
        cos0, sin0, cos1, sin1 = cos1, sin1, twice * cos1 - cos0, twice * sin1 - sin0


def kernel(spectra, slow_bins, weight_steps, delays, slowness, node_spectra, power,
           gathered, table, wide, plus, minus, beams, hats, starts, outgoing, incoming, tabs, eighth, total, sent, landed,
           mine, theirs,
           ag_send, ag_recv, tab_send, tab_recv, sum_send, sum_recv, pow_send, pow_recv):
    z, y, x = places()
    freq = lax.axis_index("freq")
    first_bin = BIN0 + freq * F
    barrier = pltpu.get_barrier_semaphore()
    greet = [cable_id(z, y, (x + 1) % X), cable_id(z, y, (x + X - 1) % X),
             cable_id(z, (y + 1) % Y, x), cable_id(z, (y + Y - 1) % Y, x)]
    greet += [cable_id((z + i) % Z, y, x) for i in range(1, Z)]
    greet += [{"freq": (freq + i) % FREQ_DEV} for i in range(1, FREQ_DEV)]
    for device in greet:
        pl.semaphore_signal(barrier, inc=1, device_id=device, device_id_type=MESH)

    own = y * X + x
    for b in range(BLOCKS):
        for c in range(2):
            block = spectra[c, b * STRIDE:(b + 1) * STRIDE, :].astype(jnp.float32).T.astype(jnp.bfloat16)
            for q in range(CHUNKS):
                rows = pl.multiple_of(own * SHARD + q * CROWS + (b * 2 + c) * CF, CF)
                gathered[pl.ds(rows, CF), :] = block[q * CF:(q + 1) * CF]
    pl.semaphore_wait(barrier, len(greet))

    half, quarter = CROWS // 2, CROWS // 4

    def shifted(way, dx, dy):
        if way == 0:
            return (y + Y + dy) % Y, (x + X + dx) % X
        return (y + Y + dx) % Y, (x + X + dy) % X

    started = []

    def transfer(q, way, stage, kind, owner):
        by = 1 if kind in (0, 2) else -1
        to = shifted(way, by, 0) if stage == 0 else shifted(way, 0, by)
        start = (owner[0] * X + owner[1]) * SHARD + q * CROWS + way * half + (quarter if kind == 3 else 0)
        piece = gathered.at[pl.ds(pl.multiple_of(start, 16), half if kind < 2 else quarter), :]
        return pltpu.make_async_remote_copy(
            src_ref=piece, dst_ref=piece,
            send_sem=ag_send.at[q, way, stage, kind], recv_sem=ag_recv.at[q, way, stage, kind],
            device_id=cable_id(z, *to), device_id_type=MESH)

    def send(q, way, stage, kind, owner):
        copy = transfer(q, way, stage, kind, owner)
        copy.start()
        started.append(copy)

    def arrive(q, way, stage, kind, owner):
        transfer(q, way, stage, kind, owner).wait_recv()

    first = {0: 0, 1: -1, 2: 1, 3: 2}

    def send_own(q):
        for stage in range(2):
            for way in range(2):
                for kind in range(2):
                    send(q, way, stage, kind, shifted(way, 0, 0))

    def from_neighbours(q):
        for way in range(2):
            for kind, j in ((0, 1), (1, 2)):
                owner = shifted(way, first[j], 0)
                arrive(q, way, 0, kind, owner)
                send(q, way, 0, 2 + kind, owner)
                send(q, way, 1 + j, 0, owner)
                send(q, way, 1 + j, 1, owner)

    def from_across(q):
        for way in range(2):
            owner = shifted(way, 2, 0)
            arrive(q, way, 0, 2, owner)
            arrive(q, way, 0, 3, owner)
            send(q, way, 4, 0, owner)
            send(q, way, 4, 1, owner)

    def pass_on(q, j):
        for way in range(2):
            for kind, by in ((0, -1), (1, 1)):
                owner = shifted(way, first[j], by)
                arrive(q, way, 1 + j, kind, owner)
                send(q, way, 1 + j, 2 + kind, owner)

    def last_pieces(q):
        for j in range(4):
            for way in range(2):
                owner = shifted(way, first[j], 2)
                arrive(q, way, 1 + j, 2, owner)
                arrive(q, way, 1 + j, 3, owner)

    def steer(part, parts):
        def one(group, carry):
            steering(group, first_bin, table)
            return carry

        lax.fori_loop(part * (F // WIDE) // parts, (part + 1) * (F // WIDE) // parts, one, 0)

    def tables_from(i):
        source = (z + Z - i) % Z
        if i == 0:
            incoming[z] = outgoing[z]
        else:
            pltpu.make_async_remote_copy(
                src_ref=outgoing.at[z], dst_ref=incoming.at[source],
                send_sem=tab_send.at[i - 1], recv_sem=tab_recv.at[i - 1],
                device_id=cable_id((z + i) % Z, y, x), device_id_type=MESH).wait_recv()
        for k in range(3):
            tabs[source, k] = incoming[source, k].astype(jnp.float32)[:PAD_ROWS]

    def prepare(m, slot):
        def one(g, carry):
            for j in range(GROUP):
                prepare_one(m, g * GROUP + j, slot, first_bin, slowness, tabs, hats, starts)
            return carry

        lax.fori_loop(0, ROWS // GROUP, one, 0)

    def stack(q, begin, end):
        def one_tile(tile, carry):
            stack_tile(q, tile, wide, table, plus, minus, beams)
            return carry

        lax.fori_loop(begin, end, one_tile, 0)

    send_own(0)
    for i, source in enumerate((slow_bins, weight_steps, delays)):
        for to in range(Z):
            if to == 0:
                head = jnp.full((1, N), -2000 if i == 0 else 0, jnp.int32)
                rows = jnp.concatenate([head, source[0:LOCAL, :]], axis=0)
            else:
                rows = source[to * LOCAL - 1:(to + 1) * LOCAL, :]
            rows = jnp.concatenate([rows, jnp.zeros((TAB_ROWS - ROWS, N), jnp.int32)], axis=0)
            outgoing[to, i] = rows.astype(jnp.int16)
    tab_copies = []
    for i in range(1, Z):
        copy = pltpu.make_async_remote_copy(
            src_ref=outgoing.at[(z + i) % Z], dst_ref=incoming.at[z],
            send_sem=tab_send.at[i - 1], recv_sem=tab_recv.at[i - 1],
            device_id=cable_id((z + i) % Z, y, x), device_id_type=MESH)
        copy.start()
        tab_copies.append(copy)
    steer(0, 4)
    from_neighbours(0)
    steer(1, 4)
    send_own(1)
    from_across(0)
    steer(2, 4)
    pass_on(0, 0)
    steer(3, 4)
    pass_on(0, 1)
    pass_on(0, 2)
    tables_from(0)
    prepare(z, 0)
    pass_on(0, 3)
    from_neighbours(1)
    for i in range(1, Z):
        tables_from(i)
    prepare((z + 1) % Z, 1)
    from_across(1)
    prepare((z + 2) % Z, 2)
    last_pieces(0)
    pass_on(1, 0)
    widen(0, gathered, wide)
    stack(0, 0, CT // 2)
    pass_on(1, 1)
    pass_on(1, 2)
    stack(0, CT // 2, CT)
    pass_on(1, 3)
    prepare((z + 3) % Z, None)
    last_pieces(1)
    widen(1, gathered, wide)
    stack(1, 0, CT)

    sums = []
    for step in range(Z):
        m = (z + 1 + step) % Z
        cos8, sin8 = unit_circle(tabs[m, 2] * 8.0, float(NT))
        eighth[0] = cos8
        eighth[1] = sin8
        total[...] = jnp.zeros_like(total)

        def one_group(g, carry):
            for j in range(GROUP):
                r = g * GROUP + j
                hat = hat_of(m, r, slowness, tabs) if step == 2 else hats[(step + 1) % Z, r]
                project_one(m, r, hat, beams, starts, eighth, total)
            return carry

        lax.fori_loop(0, ROWS // GROUP, one_group, 0)
        if step < Z - 1:
            sent[step] = total[...].astype(jnp.bfloat16)
            copy = pltpu.make_async_remote_copy(
                src_ref=sent.at[step], dst_ref=landed.at[step],
                send_sem=sum_send.at[step], recv_sem=sum_recv.at[step],
                device_id=cable_id(m, y, x), device_id_type=MESH)
            copy.start()
            sums.append(copy)

    for copy in sums:
        copy.wait_recv()
    others = (landed[0].astype(jnp.float32) + landed[1].astype(jnp.float32)) + landed[2].astype(jnp.float32)
    result = (total[...] + others) * (Z * LOCAL) ** -0.5
    mine[...] = jnp.broadcast_to(jnp.sum(result * result, axis=0, keepdims=True), (8, N))
    power_copies = []
    for i in range(1, FREQ_DEV):
        copy = pltpu.make_async_remote_copy(
            src_ref=mine, dst_ref=theirs.at[i - 1],
            send_sem=pow_send.at[i - 1], recv_sem=pow_recv.at[i - 1],
            device_id={"freq": (freq + i) % FREQ_DEV}, device_id_type=MESH)
        copy.start()
        power_copies.append(copy)
    split = result.reshape(FT, 2, 8, N)
    for c in range(2):
        part = split[:, c].reshape(F, N)
        node_spectra[:, c, :] = part.T
    for copy in power_copies:
        copy.wait_recv()
    power[...] = (mine[0:1] + theirs[0, 0:1] + theirs[1, 0:1] + theirs[2, 0:1]) * (1.0 / (F * FREQ_DEV))
    for copy in started + tab_copies + sums + power_copies:
        copy.wait_send()


def slowness_rows():
    s = np.full((256, 128), 4000.0, np.float32)
    s[0:HALF + 1] = np.arange(HALF + 1)[:, None]
    s[129:129 + HALF] = -np.arange(1, HALF + 1)[:, None]
    return jnp.asarray(s, jnp.bfloat16)


def shards(spectra, slow_bins, weight_steps, delays):
    vmem = pl.BlockSpec(memory_space=pltpu.VMEM)
    f32, bf16, dma = jnp.float32, jnp.bfloat16, pltpu.SemaphoreType.DMA
    node_spectra, power = pl.pallas_call(
        kernel,
        out_shape=(jax.ShapeDtypeStruct((N, 2, F), f32), jax.ShapeDtypeStruct((1, N), f32)),
        in_specs=[vmem] * 5,
        out_specs=(vmem, vmem),
        scratch_shapes=[
            pltpu.VMEM((PLANE * SHARD, 128), bf16),
            pltpu.VMEM((F, 256, 256), bf16),
            pltpu.VMEM(((PAD_ROWS + 1) * PER, 128), f32),
            pltpu.VMEM((PAD_ROWS * STEP, 128), f32),
            pltpu.VMEM((PAD_ROWS * STEP, 128), f32),
            pltpu.VMEM((ROWS, 2 * F, 256), bf16),
            pltpu.VMEM((Z - 1, ROWS, 256, N), bf16),
            pltpu.VMEM((Z, ROWS, 16, N), f32),
            pltpu.VMEM((Z, 3, TAB_ROWS, N), jnp.int16),
            pltpu.VMEM((Z, 3, TAB_ROWS, N), jnp.int16),
            pltpu.VMEM((Z, 3, PAD_ROWS, N), f32),
            pltpu.VMEM((2, PAD_ROWS, N), f32),
            pltpu.VMEM((2 * F, N), f32),
            pltpu.VMEM((Z - 1, 2 * F, N), bf16),
            pltpu.VMEM((Z - 1, 2 * F, N), bf16),
            pltpu.VMEM((8, N), f32),
            pltpu.VMEM((FREQ_DEV - 1, 8, N), f32),
            dma((CHUNKS, 2, 5, 4)),
            dma((CHUNKS, 2, 5, 4)),
            dma((Z - 1,)),
            dma((Z - 1,)),
            dma((Z - 1,)),
            dma((Z - 1,)),
            dma((FREQ_DEV - 1,)),
            dma((FREQ_DEV - 1,)),
        ],
        compiler_params=pltpu.CompilerParams(
            collective_id=0, has_side_effects=True, vmem_limit_bytes=63 * 1024 * 1024
        ),
    )(spectra, slow_bins, weight_steps, delays, slowness_rows())
    return node_spectra, power.reshape(N)


def solution(mesh):
    placed = (P(None, "cable", "freq"), P(None, "cable"), P(None, "cable"), P(None, "cable"))
    return jax.shard_map(
        shards,
        mesh=mesh,
        in_specs=placed,
        out_specs=(P("cable", None, "freq"), P("cable")),
        check_vma=False,
    )
```

time: 83.7 us -> 68.9 us (0.82)
  the two profiles are of different devices: /device:TPU:33 before, /device:TPU:1 now
where the time goes in v2:
time: 68.9 us; the launch traced here: 68.8 us
  Pallas kernels  65.9 us (96%)
  local copies, waits for them, and re-layouts  2.24 us (3%)
    pallas_call x1, Pallas kernels, shards(): pl.pallas_call(kernel, out_shape=(jax.ShapeDtypeStruct((N, 2, F), f32), j...  65.9 us
    unnamed x4, local copies, waits for them, and re-layouts  2.24 us

profile of v2, /device:TPU:1, one launch (start us, length us, event | category | flops | bytes accessed | tf_op | source)
XLA Modules:
  0.0 68.8 jit_solution(18247495543003375593)
XLA Ops:
  0.6 65.9 %shard_map.68 = (f32[256,2,128]{2,1,0:T(2,128)}, f32[1,256]{1,0:T(1,128)}) custom-call(bf16[2,384,128]{2,1,0:T(8,128)(2,1)} %spectra.1, s32[192,256]{1,0:T(8,128)} %slow_bins.1, s32[192,256]{1,0:T(8,128)} %weight_steps.1, s32[192,256]{1,0:T(8,128)} %delays.1, bf16[256,128]{1,0:T(8,128)(2,1)} %constant.2.clone.slowness), custom_call_target="tpu_custom_call" | custom-call | tf_op jit(solution)/shard_map/pallas_call | solution.py:411
  66.5 0.0 copy-start
  66.6 1.7 %copy.9 = f32[256,2,128]{2,1,0:T(2,128)} copy(f32[256,2,128]{2,1,0:T(2,128)} %get-tuple-element.8) | data formatting | bytes 524288
  68.2 0.0 copy-done
  68.2 0.6 copy.10
Async XLA Ops:
  66.5 1.7 %copy-start = (f32[1,256]{1,0:T(1,128)S(1)}, f32[1,256]{1,0:T(1,128)}, u32[]{:S(2)}) copy-start(f32[1,256]{1,0:T(1,128)} %get-tuple-element.5) | copy-start | bytes 3076

commit v3 on v2

--- a/solution.py
+++ b/solution.py
@@ -28,11 +28,9 @@
 ROWS = LOCAL + 1
 PAD_ROWS = 56
 FT = F // 8
-CHUNKS = 2
-CF = F // CHUNKS
-CT = CF // 8
-CROWS = SHARD // CHUNKS
-PER = 2 * CF + 8
+CHUNK_BINS = (96, 32)
+CHUNKS = len(CHUNK_BINS)
+PER = 2 * max(CHUNK_BINS) + 8
 STEP = 24
 WIDE = 4
 TAB_ROWS = 64
@@ -73,6 +71,14 @@
 
 def cable_id(z, y, x):
     return {"cable": (z * Y + y) * X + x}
+
+
+def offset_of(step):
+    return 2 - step + 3 * (step // 2) - 2 * (step // 3)
+
+
+def chunk_rows(q):
+    return 2 * BLOCKS * sum(CHUNK_BINS[:q]), 2 * BLOCKS * CHUNK_BINS[q]
 
 
 def steering(group, first_bin, table):
@@ -87,7 +93,7 @@
         cos8, sin8 = unit_circle(bs * 8.0, period)
         cos0, sin0 = cos0 * factor, sin0 * factor
         state.append((cos0, sin0, cos0 * cos8 - sin0 * sin8, sin0 * cos8 + cos0 * sin8, cos8 + cos8))
-    for step in range(SUB_LEN // 16):
+    for step in range(STRIDE // 16):
         rows = pl.ds(step * 16, 16)
         for u in range(WIDE):
             cos0, sin0, cos1, sin1, twice = state[u]
@@ -98,40 +104,49 @@
             state[u] = cos0, sin0, cos1, sin1, twice
 
 
-def widen(chunk, gathered, wide):
-    wide[0:2 * CF] = jnp.zeros((2 * CF, 128), jnp.float32)
-    wide[(LOCAL + 1) * PER:(LOCAL + 1) * PER + 2 * CF] = jnp.zeros((2 * CF, 128), jnp.float32)
+def widen(q, gathered, wide):
+    base, count = chunk_rows(q)
+    size = count // BLOCKS
+    wide[0:size] = jnp.zeros((size, 128), jnp.float32)
+    wide[(LOCAL + 1) * PER:(LOCAL + 1) * PER + size] = jnp.zeros((size, 128), jnp.float32)
 
     def one(device, carry):
         for b in range(BLOCKS):
-            source = pl.multiple_of(device * SHARD + chunk * CROWS + b * 2 * CF, 2 * CF)
+            source = pl.multiple_of(device * SHARD + base + b * size, 64)
             target = pl.multiple_of((device * BLOCKS + b + 1) * PER, 8)
-            wide[pl.ds(target, 2 * CF)] = gathered[pl.ds(source, 2 * CF)].astype(jnp.float32)
+            wide[pl.ds(target, size)] = gathered[pl.ds(source, size)].astype(jnp.float32)
         return carry
 
     lax.fori_loop(0, PLANE, one, 0)
 
 
-def stack_tile(chunk, tile, wide, table, plus, minus, beams):
+def stack_tile(q, tile, first_bin, wide, table, plus, minus, beams):
+    bins = CHUNK_BINS[q]
+    before = sum(CHUNK_BINS[:q])
     for f0 in range(8):
         at = tile * 8 + f0
-        parts = []
-        for c in range(2):
-            left = wide[pl.ds(c * CF + at, PAD_ROWS, stride=PER), :]
-            right = wide[pl.ds(PER + c * CF + at, PAD_ROWS, stride=PER), :]
-            parts.append(jnp.concatenate([left, right], axis=1))
+        parts = [wide[pl.ds(c * bins + at, PAD_ROWS, stride=PER), :] for c in range(2)]
         frames = jnp.concatenate(parts, axis=0).astype(jnp.bfloat16)
-        out = jnp.dot(frames, table[chunk * CF + at], preferred_element_type=jnp.float32)
+        out = jnp.dot(frames, table[before + at], preferred_element_type=jnp.float32)
         a_re, b_re = out[:PAD_ROWS, :128], out[:PAD_ROWS, 128:]
         a_im, b_im = out[PAD_ROWS:, :128], out[PAD_ROWS:, 128:]
         plus[pl.ds(f0, PAD_ROWS, stride=STEP), :] = a_re + b_im
         plus[pl.ds(8 + f0, PAD_ROWS, stride=STEP), :] = a_im - b_re
         minus[pl.ds(f0, PAD_ROWS, stride=STEP), :] = a_re - b_im
         minus[pl.ds(8 + f0, PAD_ROWS, stride=STEP), :] = a_im + b_re
-    rows = pl.ds(pl.multiple_of((chunk * CT + tile) * 16, 16), 16)
-    for side, sorted_beams in enumerate((plus, minus)):
-        block = sorted_beams[...].reshape(PAD_ROWS, STEP, 128)[:ROWS, :16]
-        beams[:, rows, side * 128:(side + 1) * 128] = block.astype(jnp.bfloat16)
+    bin_of = first_bin + before + tile * 8 + lax.broadcasted_iota(jnp.int32, (8, 128), 0)
+    s = lax.broadcasted_iota(jnp.int32, (8, 128), 1)
+    turn_re, turn_im = unit_circle((bin_of * s * STRIDE).astype(jnp.float32), float(50 * NT))
+    rows = pl.ds(pl.multiple_of((before // 8 + tile) * 16, 16), 16)
+    for side, stacked in enumerate((plus, minus)):
+        im_part = turn_im if side == 0 else -turn_im
+        re, im = stacked[0:8, :], stacked[8:16, :]
+        for r in range(ROWS):
+            at = (r + 1) * STEP
+            next_re, next_im = stacked[at:at + 8, :], stacked[at + 8:at + 16, :]
+            both = [re + (turn_re * next_re + im_part * next_im), im + (turn_re * next_im - im_part * next_re)]
+            beams[r, rows, side * 128:(side + 1) * 128] = jnp.concatenate(both, axis=0).astype(jnp.bfloat16)
+            re, im = next_re, next_im
 
 
 def table_row(ref, r, *at):
@@ -154,8 +169,7 @@
 
 
 def prepare_one(m, r, slot, first_bin, slowness, tabs, hats, starts):
-    if slot is not None:
-        hats[slot, r] = hat_of(m, r, slowness, tabs)
+    hats[slot, r] = hat_of(m, r, slowness, tabs)
     bins = (first_bin + lax.broadcasted_iota(jnp.int32, (8, N), 0)).astype(jnp.float32)
     cos0, sin0 = unit_circle(table_row(tabs, r, m, 2) * bins, float(NT))
     starts[m, r, 0:8] = cos0
@@ -177,14 +191,15 @@
 
 def kernel(spectra, slow_bins, weight_steps, delays, slowness, node_spectra, power,
            gathered, table, wide, plus, minus, beams, hats, starts, outgoing, incoming, tabs, eighth, total, sent, landed,
-           mine, theirs,
-           ag_send, ag_recv, tab_send, tab_recv, sum_send, sum_recv, pow_send, pow_recv):
+           mine, theirs, finished,
+           ag_send, ag_recv, tab_send, tab_recv, sum_send, sum_recv, pow_send, pow_recv, out_sem):
     z, y, x = places()
     freq = lax.axis_index("freq")
     first_bin = BIN0 + freq * F
     barrier = pltpu.get_barrier_semaphore()
     greet = [cable_id(z, y, (x + 1) % X), cable_id(z, y, (x + X - 1) % X),
-             cable_id(z, (y + 1) % Y, x), cable_id(z, (y + Y - 1) % Y, x)]
+             cable_id(z, (y + 1) % Y, x), cable_id(z, (y + Y - 1) % Y, x),
+             cable_id(z, y, (x + 2) % X), cable_id(z, (y + 2) % Y, x)]
     greet += [cable_id((z + i) % Z, y, x) for i in range(1, Z)]
     greet += [{"freq": (freq + i) % FREQ_DEV} for i in range(1, FREQ_DEV)]
     for device in greet:
@@ -194,12 +209,11 @@
     for b in range(BLOCKS):
         for c in range(2):
             block = spectra[c, b * STRIDE:(b + 1) * STRIDE, :].astype(jnp.float32).T.astype(jnp.bfloat16)
-            for q in range(CHUNKS):
-                rows = pl.multiple_of(own * SHARD + q * CROWS + (b * 2 + c) * CF, CF)
-                gathered[pl.ds(rows, CF), :] = block[q * CF:(q + 1) * CF]
+            for q, bins in enumerate(CHUNK_BINS):
+                before = sum(CHUNK_BINS[:q])
+                rows = pl.multiple_of(own * SHARD + chunk_rows(q)[0] + (b * 2 + c) * bins, 32)
+                gathered[pl.ds(rows, bins), :] = block[before:before + bins]
     pl.semaphore_wait(barrier, len(greet))
-
-    half, quarter = CROWS // 2, CROWS // 4
 
     def shifted(way, dx, dy):
         if way == 0:
@@ -207,12 +221,21 @@
         return (y + Y + dx) % Y, (x + X + dy) % X
 
     started = []
+    by_kind = (1, -1, 2)
 
     def transfer(q, way, stage, kind, owner):
-        by = 1 if kind in (0, 2) else -1
-        to = shifted(way, by, 0) if stage == 0 else shifted(way, 0, by)
-        start = (owner[0] * X + owner[1]) * SHARD + q * CROWS + way * half + (quarter if kind == 3 else 0)
-        piece = gathered.at[pl.ds(pl.multiple_of(start, 16), half if kind < 2 else quarter), :]
+        base, count = chunk_rows(q)
+        start, size = base + way * (count // 2), count // 2
+        if stage == 0:
+            to = shifted(way, by_kind[kind], 0)
+        elif q == CHUNKS - 1:
+            to = shifted(way, 0, by_kind[kind])
+        else:
+            to = shifted(way, 0, by_kind[kind % 2])
+            if kind >= 2:
+                size = count // 4
+                start += size * (kind - 2)
+        piece = gathered.at[pl.ds(pl.multiple_of((owner[0] * X + owner[1]) * SHARD + start, 16), size), :]
         return pltpu.make_async_remote_copy(
             src_ref=piece, dst_ref=piece,
             send_sem=ag_send.at[q, way, stage, kind], recv_sem=ag_recv.at[q, way, stage, kind],
@@ -226,30 +249,22 @@
     def arrive(q, way, stage, kind, owner):
         transfer(q, way, stage, kind, owner).wait_recv()
 
-    first = {0: 0, 1: -1, 2: 1, 3: 2}
+    first = (0, -1, 1, 2)
 
     def send_own(q):
-        for stage in range(2):
-            for way in range(2):
-                for kind in range(2):
-                    send(q, way, stage, kind, shifted(way, 0, 0))
-
-    def from_neighbours(q):
         for way in range(2):
-            for kind, j in ((0, 1), (1, 2)):
-                owner = shifted(way, first[j], 0)
-                arrive(q, way, 0, kind, owner)
-                send(q, way, 0, 2 + kind, owner)
-                send(q, way, 1 + j, 0, owner)
-                send(q, way, 1 + j, 1, owner)
-
-    def from_across(q):
+            for kind in range(3):
+                send(q, way, 0, kind, shifted(way, 0, 0))
         for way in range(2):
-            owner = shifted(way, 2, 0)
-            arrive(q, way, 0, 2, owner)
-            arrive(q, way, 0, 3, owner)
-            send(q, way, 4, 0, owner)
-            send(q, way, 4, 1, owner)
+            for kind in range(3 if q == CHUNKS - 1 else 2):
+                send(q, way, 1, kind, shifted(way, 0, 0))
+
+    def from_first_axis(q, j):
+        for way in range(2):
+            owner = shifted(way, first[j], 0)
+            arrive(q, way, 0, j - 1, owner)
+            for kind in range(3 if q == CHUNKS - 1 else 2):
+                send(q, way, 1 + j, kind, owner)
 
     def pass_on(q, j):
         for way in range(2):
@@ -263,7 +278,11 @@
             for way in range(2):
                 owner = shifted(way, first[j], 2)
                 arrive(q, way, 1 + j, 2, owner)
-                arrive(q, way, 1 + j, 3, owner)
+                if q == CHUNKS - 1:
+                    arrive(q, way, 1 + j, 0, shifted(way, first[j], -1))
+                    arrive(q, way, 1 + j, 1, shifted(way, first[j], 1))
+                else:
+                    arrive(q, way, 1 + j, 3, owner)
 
     def steer(part, parts):
         def one(group, carry):
@@ -293,11 +312,12 @@
         lax.fori_loop(0, ROWS // GROUP, one, 0)
 
     def stack(q, begin, end):
-        def one_tile(tile, carry):
-            stack_tile(q, tile, wide, table, plus, minus, beams)
+        def four_tiles(group, carry):
+            for u in range(4):
+                stack_tile(q, group * 4 + u, first_bin, wide, table, plus, minus, beams)
             return carry
 
-        lax.fori_loop(begin, end, one_tile, 0)
+        lax.fori_loop(begin // 4, end // 4, four_tiles, 0)
 
     send_own(0)
     for i, source in enumerate((slow_bins, weight_steps, delays)):
@@ -318,62 +338,56 @@
         copy.start()
         tab_copies.append(copy)
     steer(0, 4)
-    from_neighbours(0)
     steer(1, 4)
+    from_first_axis(0, 1)
+    from_first_axis(0, 2)
+    steer(2, 4)
+    from_first_axis(0, 3)
+    pass_on(0, 0)
     send_own(1)
-    from_across(0)
-    steer(2, 4)
-    pass_on(0, 0)
     steer(3, 4)
+    tables_from(0)
     pass_on(0, 1)
+    prepare(z, 3)
     pass_on(0, 2)
-    tables_from(0)
-    prepare(z, 0)
+    from_first_axis(1, 1)
+    from_first_axis(1, 2)
+    from_first_axis(1, 3)
     pass_on(0, 3)
-    from_neighbours(1)
-    for i in range(1, Z):
-        tables_from(i)
-    prepare((z + 1) % Z, 1)
-    from_across(1)
-    prepare((z + 2) % Z, 2)
+    for step in range(Z - 1):
+        tables_from(Z - offset_of(step))
+        prepare((z + offset_of(step)) % Z, step)
     last_pieces(0)
-    pass_on(1, 0)
     widen(0, gathered, wide)
-    stack(0, 0, CT // 2)
-    pass_on(1, 1)
-    pass_on(1, 2)
-    stack(0, CT // 2, CT)
-    pass_on(1, 3)
-    prepare((z + 3) % Z, None)
+    stack(0, 0, CHUNK_BINS[0] // 8)
     last_pieces(1)
     widen(1, gathered, wide)
-    stack(1, 0, CT)
-
-    sums = []
-    for step in range(Z):
-        m = (z + 1 + step) % Z
+    stack(1, 0, CHUNK_BINS[1] // 8)
+
+    def sum_copy(step, m):
+        return pltpu.make_async_remote_copy(
+            src_ref=sent.at[step], dst_ref=landed.at[step],
+            send_sem=sum_send.at[step], recv_sem=sum_recv.at[step],
+            device_id=cable_id(m, y, x), device_id_type=MESH)
+
+    def one_step(step, carry):
+        m = (z + offset_of(step)) % Z
         cos8, sin8 = unit_circle(tabs[m, 2] * 8.0, float(NT))
         eighth[0] = cos8
         eighth[1] = sin8
         total[...] = jnp.zeros_like(total)
-
-        def one_group(g, carry):
-            for j in range(GROUP):
-                r = g * GROUP + j
-                hat = hat_of(m, r, slowness, tabs) if step == 2 else hats[(step + 1) % Z, r]
-                project_one(m, r, hat, beams, starts, eighth, total)
-            return carry
-
-        lax.fori_loop(0, ROWS // GROUP, one_group, 0)
-        if step < Z - 1:
+        for r in range(ROWS):
+            project_one(m, r, hats[step, r], beams, starts, eighth, total)
+
+        @pl.when(step < Z - 1)
+        def _():
             sent[step] = total[...].astype(jnp.bfloat16)
-            copy = pltpu.make_async_remote_copy(
-                src_ref=sent.at[step], dst_ref=landed.at[step],
-                send_sem=sum_send.at[step], recv_sem=sum_recv.at[step],
-                device_id=cable_id(m, y, x), device_id_type=MESH)
-            copy.start()
-            sums.append(copy)
-
+            sum_copy(step, m).start()
+
+        return carry
+
+    lax.fori_loop(0, Z, one_step, 0)
+    sums = [sum_copy(step, (z + offset_of(step)) % Z) for step in range(Z - 1)]
     for copy in sums:
         copy.wait_recv()
     others = (landed[0].astype(jnp.float32) + landed[1].astype(jnp.float32)) + landed[2].astype(jnp.float32)
@@ -390,12 +404,15 @@
     split = result.reshape(FT, 2, 8, N)
     for c in range(2):
         part = split[:, c].reshape(F, N)
-        node_spectra[:, c, :] = part.T
+        finished[:, c, :] = part.T
+    writing = pltpu.make_async_copy(finished, node_spectra, out_sem)
+    writing.start()
     for copy in power_copies:
         copy.wait_recv()
     power[...] = (mine[0:1] + theirs[0, 0:1] + theirs[1, 0:1] + theirs[2, 0:1]) * (1.0 / (F * FREQ_DEV))
     for copy in started + tab_copies + sums + power_copies:
         copy.wait_send()
+    writing.wait()
 
 
 def slowness_rows():
@@ -412,15 +429,15 @@
         kernel,
         out_shape=(jax.ShapeDtypeStruct((N, 2, F), f32), jax.ShapeDtypeStruct((1, N), f32)),
         in_specs=[vmem] * 5,
-        out_specs=(vmem, vmem),
+        out_specs=(pl.BlockSpec(memory_space=pl.ANY), vmem),
         scratch_shapes=[
             pltpu.VMEM((PLANE * SHARD, 128), bf16),
-            pltpu.VMEM((F, 256, 256), bf16),
-            pltpu.VMEM(((PAD_ROWS + 1) * PER, 128), f32),
+            pltpu.VMEM((F, STRIDE, 256), bf16),
+            pltpu.VMEM((PAD_ROWS * PER, 128), f32),
             pltpu.VMEM((PAD_ROWS * STEP, 128), f32),
             pltpu.VMEM((PAD_ROWS * STEP, 128), f32),
             pltpu.VMEM((ROWS, 2 * F, 256), bf16),
-            pltpu.VMEM((Z - 1, ROWS, 256, N), bf16),
+            pltpu.VMEM((Z, ROWS, 256, N), bf16),
             pltpu.VMEM((Z, ROWS, 16, N), f32),
             pltpu.VMEM((Z, 3, TAB_ROWS, N), jnp.int16),
             pltpu.VMEM((Z, 3, TAB_ROWS, N), jnp.int16),
@@ -431,6 +448,7 @@
             pltpu.VMEM((Z - 1, 2 * F, N), bf16),
             pltpu.VMEM((8, N), f32),
             pltpu.VMEM((FREQ_DEV - 1, 8, N), f32),
+            pltpu.VMEM((N, 2, F), f32),
             dma((CHUNKS, 2, 5, 4)),
             dma((CHUNKS, 2, 5, 4)),
             dma((Z - 1,)),
@@ -439,6 +457,7 @@
             dma((Z - 1,)),
             dma((FREQ_DEV - 1,)),
             dma((FREQ_DEV - 1,)),
+            dma,
         ],
         compiler_params=pltpu.CompilerParams(
             collective_id=0, has_side_effects=True, vmem_limit_bytes=63 * 1024 * 1024

time: 68.9 us -> 63.5 us (0.922)
  Pallas kernels: 65.9 us -> 60.5 us
    pallas_call x1, Pallas kernels: 65.9 us -> 60.5 us  [shards(): pl.pallas_call(kernel, out_shape=(jax.ShapeDtypeStruct((N, 2, F), f32), j...]
where the time goes in v3:
time: 63.5 us; the launch traced here: 63.4 us
  Pallas kernels  60.5 us (95%)
  local copies, waits for them, and re-layouts  2.24 us (4%)
  between operations  0.65 us (1%)
    pallas_call x1, Pallas kernels, shards(): pl.pallas_call(kernel, out_shape=(jax.ShapeDtypeStruct((N, 2, F), f32), j...  60.5 us
    unnamed x4, local copies, waits for them, and re-layouts  2.24 us

profile of v3, /device:TPU:1, one launch (start us, length us, event | category | flops | bytes accessed | tf_op | source)
XLA Modules:
  0.0 63.4 jit_solution(1004910170539641853)
XLA Ops:
  0.6 60.5 %shard_map.68 = (f32[256,2,128]{2,1,0:T(2,128)}, f32[1,256]{1,0:T(1,128)}) custom-call(bf16[2,384,128]{2,1,0:T(8,128)(2,1)} %spectra.1, s32[192,256]{1,0:T(8,128)} %slow_bins.1, s32[192,256]{1,0:T(8,128)} %weight_steps.1, s32[192,256]{1,0:T(8,128)} %delays.1, bf16[256,128]{1,0:T(8,128)(2,1)} %constant.2.clone.slowness), custom_call_target="tpu_custom_call" | custom-call | tf_op jit(solution)/shard_map/pallas_call | solution.py:428
  61.1 0.0 copy-start
  61.1 1.7 %copy.9 = f32[256,2,128]{2,1,0:T(2,128)} copy(f32[256,2,128]{2,1,0:T(2,128)} %get-tuple-element.8) | data formatting | bytes 524288
  62.8 0.0 copy-done
  62.8 0.6 copy.10
Async XLA Ops:
  61.1 1.7 %copy-start = (f32[1,256]{1,0:T(1,128)S(1)}, f32[1,256]{1,0:T(1,128)}, u32[]{:S(2)}) copy-start(f32[1,256]{1,0:T(1,128)} %get-tuple-element.5) | copy-start | bytes 3076

commit v4 on v3

--- a/solution.py
+++ b/solution.py
@@ -157,14 +157,14 @@
     def packed(value):
         return jnp.concatenate([value, value], axis=0).astype(jnp.bfloat16)
 
-    lower = packed(table_row(tabs, r, m, 0) - float(HALF))
-    weight = table_row(tabs, r, m, 1) * (1.0 / WSTEPS)
-    rising, falling = packed(1.0 - weight), packed(1.0 + weight)
+    bin_row, weight = table_row(tabs, r, m, 0), table_row(tabs, r, m, 1) * (1.0 / WSTEPS)
+    lower, upper = packed(bin_row - float(HALF)), packed(bin_row - float(HALF - 1))
+    low_part, high_part, none = packed(1.0 - weight), packed(weight), jnp.zeros((16, N), jnp.bfloat16)
     tiles = []
     for q in range(16):
         at = slowness[q * 16:(q + 1) * 16, :]
-        gap = jnp.concatenate([at, at], axis=1) - lower
-        tiles.append(jnp.maximum(jnp.minimum(gap + rising, falling - gap), jnp.bfloat16(0)))
+        at = jnp.concatenate([at, at], axis=1)
+        tiles.append(jnp.where(at == lower, low_part, jnp.where(at == upper, high_part, none)))
     return jnp.concatenate(tiles, axis=0)
 
 
@@ -330,7 +330,7 @@
             rows = jnp.concatenate([rows, jnp.zeros((TAB_ROWS - ROWS, N), jnp.int32)], axis=0)
             outgoing[to, i] = rows.astype(jnp.int16)
     tab_copies = []
-    for i in range(1, Z):
+    for i in (1, 3, 2):
         copy = pltpu.make_async_remote_copy(
             src_ref=outgoing.at[(z + i) % Z], dst_ref=incoming.at[z],
             send_sem=tab_send.at[i - 1], recv_sem=tab_recv.at[i - 1],
@@ -350,11 +350,11 @@
     pass_on(0, 1)
     prepare(z, 3)
     pass_on(0, 2)
+    pass_on(0, 3)
     from_first_axis(1, 1)
     from_first_axis(1, 2)
     from_first_axis(1, 3)
-    pass_on(0, 3)
-    for step in range(Z - 1):
+    for step in (2, 1, 0):
         tables_from(Z - offset_of(step))
         prepare((z + offset_of(step)) % Z, step)
     last_pieces(0)
@@ -401,10 +401,7 @@
             device_id={"freq": (freq + i) % FREQ_DEV}, device_id_type=MESH)
         copy.start()
         power_copies.append(copy)
-    split = result.reshape(FT, 2, 8, N)
-    for c in range(2):
-        part = split[:, c].reshape(F, N)
-        finished[:, c, :] = part.T
+    finished[...] = result
     writing = pltpu.make_async_copy(finished, node_spectra, out_sem)
     writing.start()
     for copy in power_copies:
@@ -415,6 +412,13 @@
     writing.wait()
 
 
+def turn_kernel(sums, power_row, node_spectra, power):
+    split = sums[...].reshape(FT, 2, 8, N)
+    for c in range(2):
+        node_spectra[:, c, :] = split[:, c].reshape(F, N).T
+    power[...] = power_row[...]
+
+
 def slowness_rows():
     s = np.full((256, 128), 4000.0, np.float32)
     s[0:HALF + 1] = np.arange(HALF + 1)[:, None]
@@ -425,9 +429,9 @@
 def shards(spectra, slow_bins, weight_steps, delays):
     vmem = pl.BlockSpec(memory_space=pltpu.VMEM)
     f32, bf16, dma = jnp.float32, jnp.bfloat16, pltpu.SemaphoreType.DMA
-    node_spectra, power = pl.pallas_call(
+    sums, power_row = pl.pallas_call(
         kernel,
-        out_shape=(jax.ShapeDtypeStruct((N, 2, F), f32), jax.ShapeDtypeStruct((1, N), f32)),
+        out_shape=(jax.ShapeDtypeStruct((2 * F, N), f32), jax.ShapeDtypeStruct((1, N), f32)),
         in_specs=[vmem] * 5,
         out_specs=(pl.BlockSpec(memory_space=pl.ANY), vmem),
         scratch_shapes=[
@@ -448,7 +452,7 @@
             pltpu.VMEM((Z - 1, 2 * F, N), bf16),
             pltpu.VMEM((8, N), f32),
             pltpu.VMEM((FREQ_DEV - 1, 8, N), f32),
-            pltpu.VMEM((N, 2, F), f32),
+            pltpu.VMEM((2 * F, N), f32),
             dma((CHUNKS, 2, 5, 4)),
             dma((CHUNKS, 2, 5, 4)),
             dma((Z - 1,)),
@@ -463,6 +467,12 @@
             collective_id=0, has_side_effects=True, vmem_limit_bytes=63 * 1024 * 1024
         ),
     )(spectra, slow_bins, weight_steps, delays, slowness_rows())
+    node_spectra, power = pl.pallas_call(
+        turn_kernel,
+        out_shape=(jax.ShapeDtypeStruct((N, 2, F), f32), jax.ShapeDtypeStruct((1, N), f32)),
+        in_specs=[vmem] * 2,
+        out_specs=(vmem, vmem),
+    )(sums, power_row)
     return node_spectra, power.reshape(N)
 
 

time: 63.5 us -> 62.4 us (0.983)
  local copies, waits for them, and re-layouts: 2.24 us -> 0 us
  Pallas kernels: 60.5 us -> 61.6 us
    unnamed x4 -> x0, local copies, waits for them, and re-layouts: 2.24 us -> none
    pallas_call x1 -> x2, Pallas kernels: 60.5 us -> 61.6 us  [the longest x1 59.7 us: shards(): pl.pallas_call(kernel, out_shape=(jax.ShapeDtypeStruct((2 * F, N), f32),...]
where the time goes in v4:
time: 62.4 us; the launch traced here: 62.2 us
  Pallas kernels  61.6 us (99%)
  between operations  0.64 us (1%)
    pallas_call x1, Pallas kernels, shards(): pl.pallas_call(kernel, out_shape=(jax.ShapeDtypeStruct((2 * F, N), f32),...  59.7 us
    pallas_call x1, Pallas kernels, shards(): pl.pallas_call(turn_kernel, out_shape=(jax.ShapeDtypeStruct((N, 2, F), f3...  1.87 us

profile of v4, /device:TPU:1, one launch (start us, length us, event | category | flops | bytes accessed | tf_op | source)
XLA Modules:
  0.0 62.2 jit_solution(16302355623246064501)
XLA Ops:
  0.6 59.7 %shard_map.68 = (f32[256,256]{1,0:T(8,128)}, f32[1,256]{1,0:T(1,128)}) custom-call(bf16[2,384,128]{2,1,0:T(8,128)(2,1)} %spectra.1, s32[192,256]{1,0:T(8,128)} %slow_bins.1, s32[192,256]{1,0:T(8,128)} %weight_steps.1, s32[192,256]{1,0:T(8,128)} %delays.1, bf16[256,128]{1,0:T(8,128)(2,1)} %constant.2.clone.slowness), custom_call_target="tpu_custom_call" | custom-call | tf_op jit(solution)/shard_map/pallas_call | solution.py:432
  60.4 1.9 %shard_map.69 = (f32[256,2,128]{2,1,0:T(2,128)}, f32[1,256]{1,0:T(1,128)}) custom-call(f32[256,256]{1,0:T(8,128)} %get-tuple-element.6.sums, f32[1,256]{1,0:T(1,128)} %get-tuple-element.7.power_row), custom_call_target="tpu_custom_call" | custom-call | tf_op jit(solution)/shard_map/pallas_call | solution.py:470

commit v5 on v4

--- a/solution.py
+++ b/solution.py
@@ -192,10 +192,14 @@
 def kernel(spectra, slow_bins, weight_steps, delays, slowness, node_spectra, power,
            gathered, table, wide, plus, minus, beams, hats, starts, outgoing, incoming, tabs, eighth, total, sent, landed,
            mine, theirs, finished,
-           ag_send, ag_recv, tab_send, tab_recv, sum_send, sum_recv, pow_send, pow_recv, out_sem):
+           ag_send, ag_recv, tab_send, tab_recv, sum_send, sum_recv, pow_send, pow_recv, out_sem, raw, raw_sem):
     z, y, x = places()
     freq = lax.axis_index("freq")
     first_bin = BIN0 + freq * F
+    reading = [pltpu.make_async_copy(source, raw.at[i], raw_sem.at[i])
+               for i, source in enumerate((slow_bins, weight_steps, delays))]
+    for copy in reading:
+        copy.start()
     barrier = pltpu.get_barrier_semaphore()
     greet = [cable_id(z, y, (x + 1) % X), cable_id(z, y, (x + X - 1) % X),
              cable_id(z, (y + 1) % Y, x), cable_id(z, (y + Y - 1) % Y, x),
@@ -320,13 +324,14 @@
         lax.fori_loop(begin // 4, end // 4, four_tiles, 0)
 
     send_own(0)
-    for i, source in enumerate((slow_bins, weight_steps, delays)):
+    for i, copy in enumerate(reading):
+        copy.wait()
         for to in range(Z):
             if to == 0:
                 head = jnp.full((1, N), -2000 if i == 0 else 0, jnp.int32)
-                rows = jnp.concatenate([head, source[0:LOCAL, :]], axis=0)
+                rows = jnp.concatenate([head, raw[i, 0:LOCAL, :]], axis=0)
             else:
-                rows = source[to * LOCAL - 1:(to + 1) * LOCAL, :]
+                rows = raw[i, to * LOCAL - 1:(to + 1) * LOCAL, :]
             rows = jnp.concatenate([rows, jnp.zeros((TAB_ROWS - ROWS, N), jnp.int32)], axis=0)
             outgoing[to, i] = rows.astype(jnp.int16)
     tab_copies = []
@@ -413,9 +418,9 @@
 
 
 def turn_kernel(sums, power_row, node_spectra, power):
-    split = sums[...].reshape(FT, 2, 8, N)
+    split = sums[...].reshape(FT, 2, 8, N // 2)
     for c in range(2):
-        node_spectra[:, c, :] = split[:, c].reshape(F, N).T
+        node_spectra[:, c, :] = split[:, c].reshape(F, N // 2).T
     power[...] = power_row[...]
 
 
@@ -432,7 +437,7 @@
     sums, power_row = pl.pallas_call(
         kernel,
         out_shape=(jax.ShapeDtypeStruct((2 * F, N), f32), jax.ShapeDtypeStruct((1, N), f32)),
-        in_specs=[vmem] * 5,
+        in_specs=[vmem] + [pl.BlockSpec(memory_space=pl.ANY)] * 3 + [vmem],
         out_specs=(pl.BlockSpec(memory_space=pl.ANY), vmem),
         scratch_shapes=[
             pltpu.VMEM((PLANE * SHARD, 128), bf16),
@@ -462,6 +467,8 @@
             dma((FREQ_DEV - 1,)),
             dma((FREQ_DEV - 1,)),
             dma,
+            pltpu.VMEM((3, Z * LOCAL, N), jnp.int32),
+            dma((3,)),
         ],
         compiler_params=pltpu.CompilerParams(
             collective_id=0, has_side_effects=True, vmem_limit_bytes=63 * 1024 * 1024
@@ -470,8 +477,9 @@
     node_spectra, power = pl.pallas_call(
         turn_kernel,
         out_shape=(jax.ShapeDtypeStruct((N, 2, F), f32), jax.ShapeDtypeStruct((1, N), f32)),
-        in_specs=[vmem] * 2,
-        out_specs=(vmem, vmem),
+        grid=(2,),
+        in_specs=[pl.BlockSpec((2 * F, N // 2), lambda i: (0, i)), pl.BlockSpec((1, N // 2), lambda i: (0, i))],
+        out_specs=(pl.BlockSpec((N // 2, 2, F), lambda i: (i, 0, 0)), pl.BlockSpec((1, N // 2), lambda i: (0, i))),
     )(sums, power_row)
     return node_spectra, power.reshape(N)
 

time: 62.4 us -> 62.1 us (level)
  no operation moved by 1% of the time
where the time goes in v5:
time: 62.1 us; the launch traced here: 62 us
  Pallas kernels  61.3 us (99%)
  between operations  0.64 us (1%)
    pallas_call x1, Pallas kernels, shards(): pl.pallas_call(kernel, out_shape=(jax.ShapeDtypeStruct((2 * F, N), f32),...  59.5 us
    pallas_call x1, Pallas kernels, shards(): pl.pallas_call(turn_kernel, out_shape=(jax.ShapeDtypeStruct((N, 2, F), f3...  1.88 us

profile of v5, /device:TPU:1, one launch (start us, length us, event | category | flops | bytes accessed | tf_op | source)
XLA Modules:
  0.0 62.0 jit_solution(4421034320384759578)
XLA Ops:
  0.6 59.5 %shard_map.68 = (f32[256,256]{1,0:T(8,128)}, f32[1,256]{1,0:T(1,128)}) custom-call(bf16[2,384,128]{2,1,0:T(8,128)(2,1)} %spectra.1, s32[192,256]{1,0:T(8,128)} %slow_bins.1, s32[192,256]{1,0:T(8,128)} %weight_steps.1, s32[192,256]{1,0:T(8,128)} %delays.1, bf16[256,128]{1,0:T(8,128)(2,1)} %constant.2.clone.slowness), custom_call_target="tpu_custom_call" | custom-call | tf_op jit(solution)/shard_map/pallas_call | solution.py:437
  60.1 1.9 %shard_map.69 = (f32[256,2,128]{2,1,0:T(2,128)}, f32[1,256]{1,0:T(1,128)}) custom-call(f32[256,256]{1,0:T(8,128)} %get-tuple-element.6.sums, f32[1,256]{1,0:T(1,128)} %get-tuple-element.7.power_row), custom_call_target="tpu_custom_call" | custom-call | tf_op jit(solution)/shard_map/pallas_call | solution.py:477
